TPU v7x, 256 devices: a whole 4x4x8 slice. The times are simulated.
256 devices in a mesh: struct: 64 (over y, z, core), feat: 4 (over x).
Axes of the slice: x: 4, y: 4, z: 8, core: 2. Of those that a mesh axis runs over, the one named last changes fastest.
Arguments:
- descriptors: bfloat16 [98304, 512], P('struct', 'feat'), may hold values from -1 to 1, as said below
- atom_counts: int32 [64, 32], P('struct'), may hold values from 1 to 128, 1536 in all within a row
- partner_requests: int32 [4096], P('struct'), may hold values from 0 to 31
- pair_local: int32 [98304], P('struct'), may hold values from 0 to 31
- pair_slot: int32 [98304], P('struct'), may hold values from 0 to 63
Outputs:
- weights: float32 [98304], P(('struct', 'feat'))
Inputs may be any that keep to these rules, and one draw needn't show every extreme that they name: Each row holds real-valued descriptors. `partner_requests`: entry r of a struct index's 64 requests names a structure held by struct index r. `pair_slot`: indexes the 64 requests of the pair's own struct index.
All inputs are finite; a program needn't handle non-finite values.
Results may differ from a plain program's by a relative error of at most 0.0003.
Values may be sent and summed in bfloat16 or wider, within the bound.
A program may use at most 128 MiB of HBM per device.

v0:
```python
import math

import jax
import jax.numpy as jnp
from jax import lax
from jax.sharding import PartitionSpec as P

MAXAT = 128


def lookup(values_table, positions):
    matches = positions[:, None] == jnp.arange(values_table.shape[0], dtype=jnp.int32)[None, :]
    return jnp.sum(
        jnp.where(matches, values_table[None, :], jnp.zeros_like(values_table)[None, :]), axis=1
    )


def pack_rows(descriptors, starts, counts):
    offsets = jnp.arange(MAXAT, dtype=jnp.int32)
    row_ids = starts[:, None] + offsets[None, :]
    in_range = offsets[None, :] < counts[:, None]
    gathered_rows = jnp.take(descriptors, jnp.clip(row_ids, 0, descriptors.shape[0] - 1), axis=0)
    return jnp.where(in_range[:, :, None], gathered_rows, jnp.zeros_like(gathered_rows))


def gram_tiles(left_rows, right_rows):
    products = jnp.einsum("amd,and->amn", left_rows, right_rows, preferred_element_type=jnp.float32)
    return products.reshape(products.shape[0], -1)


def square_sums(products):
    return jnp.sum(products * products, axis=1)


def per_device(descriptors, atom_counts, partner_requests, pair_local, pair_slot):
    counts = atom_counts[0]
    starts = jnp.cumsum(counts) - counts
    local_packed = pack_rows(descriptors, starts, counts)
    full_local = lax.all_gather(local_packed, "feat", axis=2, tiled=True)
    groups = lax.axis_size("struct")
    request_count = partner_requests.shape[0]
    slot_count = request_count // groups
    wanted = lax.all_to_all(
        partner_requests.reshape(groups, slot_count),
        "struct",
        split_axis=0,
        concat_axis=0,
        tiled=True,
    )
    item_count = wanted.shape[1]
    flat_wanted = wanted.reshape(-1)
    packed = jnp.take(local_packed, flat_wanted, axis=0)
    packed = packed.reshape(groups, item_count, MAXAT, packed.shape[-1])
    partner = lax.all_to_all(packed, "struct", split_axis=0, concat_axis=0, tiled=True)
    partner = partner.reshape(request_count, MAXAT, partner.shape[-1])
    partner = lax.all_gather(partner, "feat", axis=2, tiled=True)
    feat_count = lax.axis_size("feat")
    own_self = square_sums(gram_tiles(full_local, full_local))
    partner_self = square_sums(gram_tiles(partner, partner))
    quarter = pair_local.shape[0] // feat_count
    offset = lax.axis_index("feat") * quarter
    my_local = lax.dynamic_slice_in_dim(pair_local, offset, quarter)
    my_slot = lax.dynamic_slice_in_dim(pair_slot, offset, quarter)
    block_size = math.gcd(quarter, 128)

    def block_sums(index_pair):
        left_tiles = jnp.take(full_local, index_pair[0], axis=0)
        right_tiles = jnp.take(partner, index_pair[1], axis=0)
        return square_sums(gram_tiles(left_tiles, right_tiles))

    cross_sums = lax.map(
        block_sums, (my_local.reshape(-1, block_size), my_slot.reshape(-1, block_size))
    ).reshape(-1)
    left_self = lookup(own_self, my_local)
    right_self = lookup(partner_self, my_slot)
    return cross_sums / jnp.sqrt(left_self * right_self)


def solution(mesh):
    in_specs = (P("struct", "feat"), P("struct", None), P("struct"), P("struct"), P("struct"))
    out_specs = P(("struct", "feat"))
    return jax.shard_map(
        per_device, mesh=mesh, in_specs=in_specs, out_specs=out_specs, check_vma=False
    )
```

profile of v0, /device:TPU:1, one launch (start us, length us, event | category | flops | bytes accessed | tf_op | source)
XLA Modules:
  0.0 312.4 jit_solution(9486842480682660225)
XLA Ops:
  6.5 0.0 copy-start
  6.5 0.0 copy-start.5
  6.5 0.0 all-gather.4.cloned.1.call-start
  6.5 0.8 copy.16
  7.3 0.1 reduce-window.8
  7.4 0.1 reduce.3
  7.5 0.7 bitcast_subtract_fusion
  8.2 0.1 fusion.15
  8.2 0.7 iota_compare_fusion.2
  9.0 0.0 copy-done
  9.0 12.1 %gather_fusion.2 = bf16[4096,128]{1,0:T(8,128)(2,1)S(1)} fusion(bf16[1536,128]{1,0:T(8,128)(2,1)S(1)} %copy-done, s32[4096]{0:T(1024)S(1)} %fusion.15), kind=kCustom, calls=%fused_computation.2 | custom fusion | bytes 2113536 | tf_op jit(solution)/shard_map/jit(_take)/gather | solution.py:22
  21.1 2.5 select_select_fusion
  23.6 0.0 copy-start.3
  23.6 0.0 copy-start.4
  23.6 0.0 all-gather.4.cloned.1.call-update
  23.7 0.0 all-gather.6.cloned.1.call-start
  23.7 0.0 copy-done.5
  23.7 0.1 copy.17
  23.8 22.2 %all_to_all.20 = s32[64,1,1]{2,1,0:T(1,128)S(1)} all-to-all(s32[64,1,1]{2,1,0:T(1,128)S(1)} %copy.17), channel_id=1, replica_groups=mesh['struct'=64,'feat'=4] {'struct'}, dimensions={0} | all-to-all | bytes 512 | tf_op jit(solution)/shard_map/all_to_all | solution.py:43
  46.1 1.2 reduce.4
  47.3 2.2 gather_fusion.3
  49.5 0.3 fusion.13
  49.8 56.0 %all_to_all.21 = bf16[64,1,128,128]{3,2,1,0:T(8,128)(2,1)} all-to-all(bf16[64,1,128,128]{3,2,1,0:T(8,128)(2,1)S(1)} %fusion.13), channel_id=1, replica_groups=mesh['struct'=64,'feat'=4] {'struct'}, dimensions={0} | all-to-all | bytes 4194304 | tf_op jit(solution)/shard_map/all_to_all | solution.py:54
  105.7 0.0 all-gather.6.cloned.1.call-update
  105.8 0.0 copy-done.3
  105.8 0.7 dynamic_slice.14
  106.5 0.0 copy-done.4
  106.5 0.1 dynamic_slice.13
  106.5 0.1 dynamic-slice_bitcast_fusion
  106.6 0.1 dynamic-slice_bitcast_fusion.1
  106.7 0.0 all-gather.4.cloned.1.call-done
  106.7 4.8 %multiply_reduce_fusion.2 = f32[32]{0:T(128)S(1)} fusion(bf16[32,128,512]{2,1,0:T(8,128)(2,1)} %all-gather.4.cloned.1.call-done), kind=kOutput, calls=%fused_computation.27 | convolution fusion | flops 537919488 | bytes 4194432 | tf_op jit(solution)/shard_map/amd,and->amn/dot_general | solution.py:27
  111.5 0.7 select_reduce_fusion.1
  112.2 79.0 %all-gather.6.cloned.1.call-done = bf16[64,1,128,512]{3,2,0,1:T(8,128)(2,1)} async-done(((bf16[64,1,128,128]{3,2,0,1:T(8,128)(2,1)}), bf16[64,1,128,512]{3,2,0,1:T(8,128)(2,1)}) %all-gather.6.cloned.1.call-update) | async-done | bytes 8388624 | tf_op jit(solution)/shard_map/all_gather | solution.py:56
  191.2 105.4 %while.10 = (s32[]{:T(128)}, f32[3,128]{1,0:T(4,128)S(1)}, s32[3,128]{1,0:T(4,128)S(1)}, bf16[32,128,512]{2,1,0:T(8,128)(2,1)}, s32[3,128]{1,0:T(4,128)S(1)}, /*...) while((s32[]{:T(128)}, f32[3,128]{1,0:T(4,128)S(1)}, s32[3,128]{1,0:T(4,128)S(1)}, ...), condition=%wide.region_3.4_spmd, body=%wide.region_1.3_spmd.sunk | while | flops 2168459520 | bytes 100678744 | solution.py:71
  191.2 11.7 %gather_fusion = bf16[128,128,512]{2,1,0:T(8,128)(2,1)} fusion(bf16[64,128,512]{2,1,0:T(8,128)(2,1)} %get-tuple-element.122, s32[1024]{0:T(1024)S(1)} %pad_clamp_fusion.5), kind=kCustom, calls=%fused_computation.1.clone.1 | custom fusion | bytes 33554944 | tf_op jit(solution)/shard_map/while/body/eval_jaxpr/jit(_take)/gather | solution.py:68
  202.9 10.4 %gather_fusion.1 = bf16[128,128,512]{2,1,0:T(8,128)(2,1)} fusion(bf16[32,128,512]{2,1,0:T(8,128)(2,1)} %get-tuple-element.120, s32[1024]{0:T(1024)S(1)} %pad_clamp_fusion.6), kind=kCustom, calls=%fused_computation.clone.1 | custom fusion | bytes 33554944 | tf_op jit(solution)/shard_map/while/body/eval_jaxpr/jit(_take)/gather | solution.py:67
  213.3 12.9 %multiply_reduce_fusion.4 = f32[128]{0:T(128)S(1)} fusion(bf16[128,128,512]{2,1,0:T(8,128)(2,1)} %gather_fusion, pred[128]{0:T(512)(128)(4,1)S(1)} %get-tuple-element.98, bf16[128,128,512]{2,1,0:T(8,128)(2,1)} %gather_fusion.1, pred[128]{0:T(512)(128)(4,1)S(1)} %get-tuple-element.100), kind=kOutput, calls=%fused_computation.9.clone.1 | convolution fusion | flops 2168455168 | bytes 33555200 | tf_op jit(solution)/shard_map/while/body/eval_jaxpr/amd,and->amn/dot_general | solution.py:27
  226.3 11.7 %gather_fusion = bf16[128,128,512]{2,1,0:T(8,128)(2,1)} fusion(bf16[64,128,512]{2,1,0:T(8,128)(2,1)} %get-tuple-element.122, s32[1024]{0:T(1024)S(1)} %pad_clamp_fusion.5), kind=kCustom, calls=%fused_computation.1.clone.1 | custom fusion | bytes 33554944 | tf_op jit(solution)/shard_map/while/body/eval_jaxpr/jit(_take)/gather | solution.py:68
  238.0 10.4 %gather_fusion.1 = bf16[128,128,512]{2,1,0:T(8,128)(2,1)} fusion(bf16[32,128,512]{2,1,0:T(8,128)(2,1)} %get-tuple-element.120, s32[1024]{0:T(1024)S(1)} %pad_clamp_fusion.6), kind=kCustom, calls=%fused_computation.clone.1 | custom fusion | bytes 33554944 | tf_op jit(solution)/shard_map/while/body/eval_jaxpr/jit(_take)/gather | solution.py:67
  248.4 13.0 %multiply_reduce_fusion.4 = f32[128]{0:T(128)S(1)} fusion(bf16[128,128,512]{2,1,0:T(8,128)(2,1)} %gather_fusion, pred[128]{0:T(512)(128)(4,1)S(1)} %get-tuple-element.98, bf16[128,128,512]{2,1,0:T(8,128)(2,1)} %gather_fusion.1, pred[128]{0:T(512)(128)(4,1)S(1)} %get-tuple-element.100), kind=kOutput, calls=%fused_computation.9.clone.1 | convolution fusion | flops 2168455168 | bytes 33555200 | tf_op jit(solution)/shard_map/while/body/eval_jaxpr/amd,and->amn/dot_general | solution.py:27
  261.4 11.7 %gather_fusion = bf16[128,128,512]{2,1,0:T(8,128)(2,1)} fusion(bf16[64,128,512]{2,1,0:T(8,128)(2,1)} %get-tuple-element.122, s32[1024]{0:T(1024)S(1)} %pad_clamp_fusion.5), kind=kCustom, calls=%fused_computation.1.clone.1 | custom fusion | bytes 33554944 | tf_op jit(solution)/shard_map/while/body/eval_jaxpr/jit(_take)/gather | solution.py:68
  273.1 10.5 %gather_fusion.1 = bf16[128,128,512]{2,1,0:T(8,128)(2,1)} fusion(bf16[32,128,512]{2,1,0:T(8,128)(2,1)} %get-tuple-element.120, s32[1024]{0:T(1024)S(1)} %pad_clamp_fusion.6), kind=kCustom, calls=%fused_computation.clone.1 | custom fusion | bytes 33554944 | tf_op jit(solution)/shard_map/while/body/eval_jaxpr/jit(_take)/gather | solution.py:67
  283.6 13.0 %multiply_reduce_fusion.4 = f32[128]{0:T(128)S(1)} fusion(bf16[128,128,512]{2,1,0:T(8,128)(2,1)} %gather_fusion, pred[128]{0:T(512)(128)(4,1)S(1)} %get-tuple-element.98, bf16[128,128,512]{2,1,0:T(8,128)(2,1)} %gather_fusion.1, pred[128]{0:T(512)(128)(4,1)S(1)} %get-tuple-element.100), kind=kOutput, calls=%fused_computation.9.clone.1 | convolution fusion | flops 2168455168 | bytes 33555200 | tf_op jit(solution)/shard_map/while/body/eval_jaxpr/amd,and->amn/dot_general | solution.py:27
  296.6 0.0 copy-start.1
  296.6 0.0 copy-start.2
  296.6 8.2 %multiply_reduce_fusion.1 = f32[64]{0:T(128)S(1)} fusion(bf16[64,1,128,512]{3,2,0,1:T(8,128)(2,1)} %bitcast.53), kind=kOutput, calls=%fused_computation.24 | convolution fusion | flops 1075838976 | bytes 8388864 | tf_op jit(solution)/shard_map/amd,and->amn/dot_general | solution.py:27
  304.8 0.0 copy-done.1
  304.9 0.1 select_reduce_fusion
  304.9 0.0 copy-done.2
  305.0 0.6 bitcast_multiply_fusion
  (19 shorter events, 0.2 us)
Async XLA Ops:
  6.5 2.5 copy-start
  6.5 17.2 %copy-start.5 = (s32[64]{0:T(128)S(1)}, s32[64]{0:T(128)}, u32[]{:S(2)}) copy-start(s32[64]{0:T(128)} %param.9) | copy-start | bytes 772
  6.5 100.1 %all-gather.4.cloned.1.call-start = ((), (), s32[]{:S(2)}) async-start(), calls=%async_computation.2 | async-start | bytes 5242880 | tf_op jit(solution)/shard_map/all_gather | solution.py:39
  23.6 82.1 %copy-start.3 = (s32[1536]{0:T(1024)S(1)}, s32[1536]{0:T(1024)}, u32[]{:S(2)}) copy-start(s32[1536]{0:T(1024)} %param.11) | copy-start | bytes 18436
  23.6 82.8 %copy-start.4 = (s32[1536]{0:T(1024)S(1)}, s32[1536]{0:T(1024)}, u32[]{:S(2)}) copy-start(s32[1536]{0:T(1024)} %param.10) | copy-start | bytes 18436
  23.7 167.5 %all-gather.6.cloned.1.call-start = ((), (), s32[]{:S(2)}) async-start(), calls=%async_computation.3 | async-start | bytes 10485760 | tf_op jit(solution)/shard_map/all_gather | solution.py:56
  296.6 8.3 %copy-start.1 = (s32[384]{0:T(512)S(1)}, s32[384]{0:T(512)}, u32[]{:S(2)}) copy-start(s32[384]{0:T(512)} %dynamic_slice.14) | copy-start | bytes 4612
  296.6 8.3 %copy-start.2 = (f32[384]{0:T(512)S(1)}, f32[384]{0:T(512)}, u32[]{:S(2)}) copy-start(f32[384]{0:T(512)} %select_reduce_fusion.1) | copy-start | bytes 4612
Sparse Core Ops, SparseCore 0:
  23.8 57.4 all-gather.3
  105.9 85.2 all-gather.5
where the time goes:
time: 313 us; the launch traced here: 312 us
  local copies, waits for them, and re-layouts  82.5 us (26%)
  waiting for transfers between devices  79 us (25%)
  blocking collectives  78.2 us (25%)
  matrix products  51.9 us (17%)
  between operations  13.5 us (4%)
  other arithmetic  7.09 us (2%)
    all_gather x1, waiting for transfers between devices, per_device(): partner = lax.all_gather(partner, 'feat', axis=2, tiled=True)  79 us
    all_to_all x1, blocking collectives, per_device(): lax.all_to_all(packed, 'struct', split_axis=0, concat_axis=0, tiled=True)  56 us
    dot_general x5, matrix products, gram_tiles(): jnp.einsum('amd,and->amn', left_rows, right_rows, preferred_element_type=...  51.9 us
    gather x3, local copies, waits for them, and re-layouts, block_sums(): right_tiles = jnp.take(partner, index_pair[1], axis=0)  35 us
    gather x3, local copies, waits for them, and re-layouts, block_sums(): left_tiles = jnp.take(full_local, index_pair[0], axis=0)  31.3 us
    all_to_all x1, blocking collectives, per_device(): lax.all_to_all(partner_requests.reshape(groups, slot_count), 'struct', sp...  22.2 us
    gather x1, local copies, waits for them, and re-layouts, pack_rows(): jnp.take(descriptors, jnp.clip(row_ids, 0, descriptors.shape[0] - 1), axi...  12.1 us
  transfers between devices with their start and end apart: 2, of which 1 were waited for; matrix products, arithmetic and copies ran while one was open for 3% of the time, Pallas kernels for 0%

commit v1 on v0

v1 whole, which is shorter than its diff:
```python
import jax
import jax.numpy as jnp
from jax import lax
from jax.experimental import pallas as pl
from jax.experimental.pallas import tpu as pltpu
from jax.sharding import PartitionSpec as P

MAXAT = 128
ATOMS_DEV = 1536
STRUCTS = 32
F = 4
NY, NZ, NC = 4, 8, 2
FEATS = 128
DEPTH = F * FEATS
ROWS = ATOMS_DEV // F
TILE = MAXAT // F
SPOTS = NY * NC
CHUNKS = 4
CHUNK = ROWS // CHUNKS
PAIRS = 384
MESH = pl.DeviceIdType.MESH
BF16, F32 = jnp.bfloat16, jnp.float32

NEAR = [(dy, dc) for dy in range(NY) for dc in range(NC)]
NT = (((1,), (1,)), ((), ()))


def iota(shape, dim):
    return lax.broadcasted_iota(jnp.int32, shape, dim)


def fiota(shape, dim):
    return iota(shape, dim).astype(F32)


def dot(a, b):
    return jnp.dot(a, b, preferred_element_type=F32)


def split3(x):
    high = x.astype(BF16)
    rest = x - high.astype(F32)
    middle = rest.astype(BF16)
    return high, middle, (rest - middle.astype(F32)).astype(BF16)


def kernel(x_ref, counts_ref, req_ref, local_ref, slot_ref, out_ref,
           rows, ring, stage, recv, info, asked, sizes, sums, own_self, near_self, plane_self,
           far_self, table, tables,
           x_send, x_recv, xr_send, xr_recv, z_send, z_recv, a_send, a_recv, c_send, c_recv,
           y_send, y_recv, s_send, s_recv, p_send, p_recv, t_send, t_recv):
    s = lax.axis_index("struct")
    f = lax.axis_index("feat")
    y, z, c = s // (NZ * NC), lax.rem(s // NC, NZ), lax.rem(s, NC)
    ff = f.astype(F32)

    def struct_at(dz, dy, dc):
        return (lax.rem(y + dy + NY, NY) * NZ + lax.rem(z + dz + NZ, NZ)) * NC + lax.rem(c + dc, NC)

    def at(dz, dy, dc):
        return {"struct": struct_at(dz, dy, dc)}

    def copy(src, dst, send, recv_sem, to):
        made = pltpu.make_async_remote_copy(
            src_ref=src, dst_ref=dst, send_sem=send, recv_sem=recv_sem, device_id=to,
            device_id_type=MESH)
        made.start()
        return made

    sent = []
    peers = [at(0, dy, dc) for dy, dc in NEAR[1:]]
    peers += [at(dz, dy, dc) for dz in (1, -1) for dy, dc in NEAR]
    peers += [at(dz, 0, 0) for dz in (2, 3, 4, -3, -2)]
    peers += [{"feat": lax.rem(f + d, F)} for d in range(1, F)]
    barrier = pltpu.get_barrier_semaphore()
    for peer in peers:
        pl.semaphore_signal(barrier, inc=1, device_id=peer, device_id_type=MESH)

    step = 2 * FEATS
    part = step // F
    r, q = iota((step, step), 0), iota((step, step), 1)
    wanted = F * lax.rem(r, part) + lax.rem(r // part + f, F)
    deal = jnp.where(q == wanted, 1.0, 0.0).astype(BF16)
    for b in range(ATOMS_DEV // step):
        dealt = dot(deal, x_ref[b * step:(b + 1) * step, :]).astype(BF16)
        for e in range(F):
            rows[e, b * part:(b + 1) * part, 0:FEATS] = dealt[e * part:(e + 1) * part, :]

    counts_row = jnp.concatenate(
        [counts_ref[...].astype(F32), jnp.zeros((1, 128 - STRUCTS), F32)], axis=1)
    req_row = jnp.concatenate(
        [req_ref[...].reshape(1, NY * NZ * NC).astype(F32), jnp.zeros((1, 64), F32)], axis=1)
    sub, lane = iota((STRUCTS, 128), 0), iota((STRUCTS, 128), 1)
    counts_col = jnp.sum(jnp.where(sub == lane, counts_row, 0.0), axis=1, keepdims=True)
    starts_row = jnp.sum(jnp.where(sub < lane, counts_col, 0.0), axis=0, keepdims=True)
    starts_col = jnp.sum(jnp.where(lane < sub, counts_row, 0.0), axis=1, keepdims=True)
    info[...] = jnp.concatenate(
        [req_row, counts_row, starts_row, jnp.zeros((5, 128), F32)], axis=0)

    pl.semaphore_wait(barrier, len(peers))

    first = {}
    for ch in range(CHUNKS):
        part_rows = pl.ds(ch * CHUNK, CHUNK)
        for d in range(1, F):
            first[d, ch] = copy(
                rows.at[d, part_rows, pl.ds(0, FEATS)],
                rows.at[0, part_rows, pl.ds((F - d) * FEATS, FEATS)],
                x_send.at[d - 1, ch], x_recv.at[d - 1, ch], {"feat": lax.rem(f + d, F)})
    asks = {}
    for dz, spots in ((0, range(1, SPOTS)), (1, range(0, SPOTS, 2)), (-1, range(1, SPOTS, 2))):
        for t in spots:
            dy, dc = NEAR[t]
            asks[dz, t] = copy(info, asked.at[dz % 3, t], a_send.at[dz % 3, t], a_recv.at[dz % 3, t],
                               at(-dz, -dy, dc))
    size_copies = {}
    for o in (1, 2, 3, 5, 6, 7):
        size_copies[o] = copy(info, sizes.at[o], c_send.at[o], c_recv.at[o], at(o, 0, 0))
    rest = {}
    for e in range(1, F):
        for d in range(1, F):
            rest[d, e] = copy(
                rows.at[(e + d) % F, :, pl.ds(0, FEATS)],
                rows.at[e, :, pl.ds((F - d) * FEATS, FEATS)],
                xr_send.at[d - 1, e - 1], xr_recv.at[d - 1, e - 1], {"feat": lax.rem(f + d, F)})

    hops = {}

    def hop(o, to, ch):
        src = rows.at[0] if o == 0 else ring.at[o]
        dst = (o + to) % NZ
        part_rows = pl.ds(ch * CHUNK, CHUNK)
        hops[dst, ch] = copy(src.at[part_rows], ring.at[dst, part_rows],
                             z_send.at[dst, ch], z_recv.at[dst, ch], at(to, 0, 0))

    for ch in range(CHUNKS):
        for d in range(1, F):
            first[d, ch].wait_recv()
        hop(0, 1, ch)
        hop(0, -1, ch)

    for t in range(1, SPOTS):
        asks[0, t].wait_recv()
    near_asks = jnp.concatenate([info[0:1, :]] + [asked[0, t, 0:1, :] for t in range(1, SPOTS)], axis=0)

    def cut(block, sizes_ref, o, asks_rows):
        n = asks_rows.shape[0]
        lanes = iota((n, 128), 1)
        holder = struct_at(-o, 0, 0)
        asked_for = jnp.sum(jnp.where(lanes == holder, asks_rows, 0.0), axis=1, keepdims=True)
        chosen = lanes.astype(F32) == asked_for
        count = jnp.sum(jnp.where(chosen, sizes_ref[1:2, :], 0.0), axis=1, keepdims=True)
        start = jnp.sum(jnp.where(chosen, sizes_ref[2:3, :], 0.0), axis=1, keepdims=True)
        begin = jnp.floor((start - ff + 3.0) * 0.25)
        end = jnp.floor((start + count - ff + 3.0) * 0.25)
        begin = jnp.broadcast_to(begin, (n, ROWS))
        end = jnp.broadcast_to(end, (n, ROWS))
        i, k = fiota((TILE, ROWS), 0), fiota((TILE, ROWS), 1)
        picks = [jnp.where((begin[t:t + 1] + i == k) & (k < end[t:t + 1]), 1.0, 0.0).astype(BF16)
                 for t in range(n)]
        return dot(jnp.concatenate(picks, axis=0), block).astype(BF16)

    tiles = {}

    def serve(o):
        block = rows[0] if o == 0 else ring[o]
        if o not in (0, 3, 5):
            size_copies[o].wait_recv()
        made = cut(block, info if o == 0 else sizes.at[o], o, near_asks)
        stage[o] = made
        recv[o, 0:TILE, :] = made[0:TILE, :]
        for t in range(1, SPOTS):
            dy, dc = NEAR[t]
            part_rows = pl.ds(t * TILE, TILE)
            tiles[o, t] = copy(stage.at[o, part_rows], recv.at[o, part_rows],
                               y_send.at[o, t], y_recv.at[o, t], at(0, dy, dc))

    def serve_far(o, dz):
        spots = range(0, SPOTS, 2) if dz == 1 else range(1, SPOTS, 2)
        for t in spots:
            asks[dz, t].wait_recv()
        far_asks = jnp.concatenate([asked[dz % 3, t, 0:1, :] for t in spots], axis=0)
        size_copies[o].wait_recv()
        made = cut(ring[o], sizes.at[o], o, far_asks)
        for n, t in enumerate(spots):
            part_rows = pl.ds(t * TILE, TILE)
            dy, dc = NEAR[t]
            stage[4, part_rows, :] = made[n * TILE:(n + 1) * TILE, :]
            tiles[4, t] = copy(stage.at[4, part_rows], recv.at[4, part_rows],
                               y_send.at[4, t], y_recv.at[4, t], at(dz, dy, dc))

    def products(o):
        for t in range(0 if o == 4 else 1, SPOTS):
            tiles[o, t].wait_recv()

        def one(e, carry):
            p = lax.dot_general(recv[o], rows[e], NT, preferred_element_type=F32)
            sums[e, o * SPOTS:(o + 1) * SPOTS, :] = jnp.sum(
                (p * p).reshape(SPOTS, TILE, ROWS), axis=1)
            return carry

        lax.fori_loop(0, F, one, 0)

    serve(0)
    for o in (1, 2):
        for ch in range(CHUNKS):
            hops[o, ch].wait_recv()
            hop(o, 1, ch)
            hops[NZ - o, ch].wait_recv()
            hop(NZ - o, -1, ch)
        serve(o)
        serve(NZ - o)

    for copied in rest.values():
        copied.wait_recv()

    ends_row = starts_row + counts_row
    own_row = F * fiota((ROWS, 128), 0) + ff
    own_seg = jnp.sum(jnp.where((ends_row <= own_row) & (iota((ROWS, 128), 1) < STRUCTS), 1.0, 0.0),
                      axis=1, keepdims=True)

    def members(e):
        index = F * iota((STRUCTS, ROWS), 1) + lax.rem(f + e, F)
        index = index.astype(F32)
        return (starts_col <= index) & (index < starts_col + counts_col)

    def self_part(e, total):
        inside = members(e)
        seg = jnp.sum(jnp.where(inside, fiota((STRUCTS, ROWS), 0), 0.0), axis=0, keepdims=True)
        p = lax.dot_general(rows[0], rows[e], NT, preferred_element_type=F32)
        p = jnp.where(own_seg == seg, p, 0.0)
        by_column = jnp.sum(p * p, axis=0, keepdims=True)
        return total + jnp.sum(jnp.where(inside, by_column, 0.0), axis=1, keepdims=True)

    self_col = lax.fori_loop(0, F, self_part, jnp.zeros((STRUCTS, 1), F32))
    self_row = jnp.sum(jnp.where(sub == lane, self_col, 0.0), axis=0, keepdims=True)
    own_self[...] = jnp.broadcast_to(self_row, (8, 128))
    self_copies = {}
    for t in range(1, SPOTS):
        dy, dc = NEAR[t]
        self_copies[t] = copy(own_self, near_self.at[t], s_send.at[t], s_recv.at[t], at(0, dy, dc))

    products(0)
    for t in range(1, SPOTS):
        self_copies[t].wait_recv()
    plane_self[...] = jnp.concatenate(
        [own_self[0:1, :]] + [near_self[t, 0:1, :] for t in range(1, SPOTS)], axis=0)
    plane_copies = {}
    for o in range(1, NZ):
        plane_copies[o] = copy(plane_self, far_self.at[o], p_send.at[o], p_recv.at[o], at(o, 0, 0))
    products(1)
    products(7)

    for ch in range(CHUNKS):
        hops[3, ch].wait_recv()
    serve_far(3, 1)
    for ch in range(CHUNKS):
        hops[5, ch].wait_recv()
    serve_far(5, -1)
    serve(3)
    serve(5)
    products(2)
    products(6)

    holders = NZ * SPOTS
    spot = iota((holders, 128), 0)
    o_of, t_of = spot // SPOTS, lax.rem(spot, SPOTS)
    holder_col = (lax.rem(y - t_of // NC + NY, NY) * NZ + lax.rem(z - o_of + NZ, NZ)) * NC + lax.rem(
        c + lax.rem(t_of, NC), NC)
    lanes = iota((holders, 128), 1)
    my_request = jnp.sum(jnp.where(lanes == holder_col, info[0:1, :], 0.0), axis=1, keepdims=True)
    for o in range(1, NZ):
        plane_copies[o].wait_recv()
    all_self = jnp.concatenate([plane_self[...]] + [far_self[o] for o in range(1, NZ)], axis=0)
    partner_self = jnp.sum(jnp.where(lanes.astype(F32) == my_request, all_self, 0.0), axis=1, keepdims=True)
    partner_row = jnp.sum(jnp.where(lanes == spot, partner_self, 0.0), axis=0, keepdims=True)

    products(3)
    products(5)
    products(4)

    def by_structure(e, total):
        inside = jnp.where(members(e), 1.0, 0.0).astype(BF16)
        for piece in split3(sums[e]):
            total = total + lax.dot_general(inside, piece, NT, preferred_element_type=F32)
        return total

    cross = lax.fori_loop(0, F, by_structure, jnp.zeros((STRUCTS, holders), F32))
    cross = jnp.concatenate([cross, jnp.broadcast_to(self_col, (STRUCTS, 128 - holders))], axis=1)
    table[...] = jnp.concatenate([cross, jnp.broadcast_to(partner_row, (8, 128))], axis=0)
    table_copies = [
        copy(table, tables.at[d - 1], t_send.at[d - 1], t_recv.at[d - 1], {"feat": lax.rem(f + d, F)})
        for d in range(1, F)]

    slot = slot_ref[pl.ds(pl.multiple_of(f * PAIRS, 128), PAIRS)].reshape(1, PAIRS)
    local = local_ref[pl.ds(pl.multiple_of(f * PAIRS, 128), PAIRS)].reshape(1, PAIRS)
    spot = iota((128, PAIRS), 0)
    o_of, t_of = spot // SPOTS, lax.rem(spot, SPOTS)
    holder_col = (lax.rem(y - t_of // NC + NY, NY) * NZ + lax.rem(z + NZ - lax.rem(o_of, NZ), NZ)) * NC + lax.rem(
        c + lax.rem(t_of, NC), NC)
    slot_pick = jnp.where((holder_col == slot) & (spot < holders), 1.0, 0.0).astype(BF16)
    local_pick = iota((STRUCTS, PAIRS), 0) == local

    for copied in table_copies:
        copied.wait_recv()
    total = (table[...] + tables[0]) + (tables[1] + tables[2])
    picked = sum(dot(piece, slot_pick) for piece in split3(total))
    left_self = jnp.sum(jnp.where(local_pick, total[0:STRUCTS, holders:holders + 1], 0.0), axis=0, keepdims=True)
    value = jnp.sum(jnp.where(local_pick, picked[0:STRUCTS], 0.0), axis=0, keepdims=True)
    right_self = picked[STRUCTS:STRUCTS + 1]
    out_ref[...] = (value / jnp.sqrt(left_self * right_self)).reshape(PAIRS)

    for copied in (*first.values(), *rest.values(), *asks.values(), *size_copies.values(), *hops.values(),
                   *tiles.values(), *self_copies.values(), *plane_copies.values(), *table_copies):
        copied.wait_send()


def per_device(descriptors, atom_counts, partner_requests, pair_local, pair_slot):
    dma = pltpu.SemaphoreType.DMA
    vmem = pltpu.VMEM
    pairs_of = lambda shape: [dma(shape), dma(shape)]
    return pl.pallas_call(
        kernel,
        out_shape=jax.ShapeDtypeStruct((PAIRS,), F32),
        in_specs=[pl.BlockSpec(memory_space=vmem)] * 5,
        out_specs=pl.BlockSpec(memory_space=vmem),
        scratch_shapes=[
            vmem((F, ROWS, DEPTH), BF16),
            vmem((NZ, ROWS, DEPTH), BF16),
            vmem((NZ, SPOTS * TILE, DEPTH), BF16),
            vmem((NZ, SPOTS * TILE, DEPTH), BF16),
            vmem((8, 128), F32),
            vmem((3, SPOTS, 8, 128), F32),
            vmem((NZ, 8, 128), F32),
            vmem((F, NZ * SPOTS, ROWS), F32),
            vmem((8, 128), F32),
            vmem((SPOTS, 8, 128), F32),
            vmem((8, 128), F32),
            vmem((NZ, 8, 128), F32),
            vmem((STRUCTS + 8, 128), F32),
            vmem((F - 1, STRUCTS + 8, 128), F32),
            *pairs_of((F - 1, CHUNKS)),
            *pairs_of((F - 1, F - 1)),
            *pairs_of((NZ, CHUNKS)),
            *pairs_of((3, SPOTS)),
            *pairs_of((NZ,)),
            *pairs_of((NZ, SPOTS)),
            *pairs_of((SPOTS,)),
            *pairs_of((NZ,)),
            *pairs_of((F - 1,)),
        ],
        compiler_params=pltpu.CompilerParams(
            collective_id=0, has_side_effects=True, vmem_limit_bytes=40 * 1024 * 1024),
    )(descriptors, atom_counts, partner_requests, pair_local, pair_slot)


def solution(mesh):
    in_specs = (P("struct", "feat"), P("struct", None), P("struct"), P("struct"), P("struct"))
    out_specs = P(("struct", "feat"))
    return jax.shard_map(
        per_device, mesh=mesh, in_specs=in_specs, out_specs=out_specs, check_vma=False)
```

time: 313 us -> 69.4 us (0.22)
  waiting for transfers between devices: 79 us -> 0 us
  local copies, waits for them, and re-layouts: 82.5 us -> 4.28 us
  blocking collectives: 78.2 us -> 0 us
  Pallas kernels: 0 us -> 64.9 us
  matrix products: 51.9 us -> 0 us
  between operations: 13.5 us -> 0.01 us
  other arithmetic: 7.09 us -> 0 us
    gather x8 -> x0, local copies, waits for them, and re-layouts: 80.6 us -> none  [the longest x3 35 us: block_sums(): right_tiles = jnp.take(partner, index_pair[1], axis=0)]
    all_gather x2 -> x0, waiting for transfers between devices: 79 us -> none  [the longest x1 79 us: per_device(): partner = lax.all_gather(partner, 'feat', axis=2, tiled=True)]
    all_to_all x2 -> x0, blocking collectives: 78.2 us -> none  [the longest x1 56 us: per_device(): lax.all_to_all(packed, 'struct', split_axis=0, concat_axis=0, tiled=True)]
    pallas_call x0 -> x1, Pallas kernels: none -> 64.9 us  [per_device(): pl.pallas_call(kernel, out_shape=jax.ShapeDtypeStruct((PAIRS,), F32), in_...]
    dot_general x5 -> x0, matrix products: 51.9 us -> none  [gram_tiles(): jnp.einsum('amd,and->amn', left_rows, right_rows, preferred_element_type=...]
    unnamed x12 -> x11, local copies, waits for them, and re-layouts: 0.03 us -> 4.28 us
  transfers between devices with their start and end apart: 2 -> 0, of which waited for: 1 -> 0; matrix products, arithmetic and copies ran while one was open for 3% -> 0% of each run, Pallas kernels for 0% -> 0%
where the time goes in v1:
time: 69.4 us; the launch traced here: 69.2 us
  Pallas kernels  64.9 us (94%)
  local copies, waits for them, and re-layouts  4.28 us (6%)
    pallas_call x1, Pallas kernels, per_device(): pl.pallas_call(kernel, out_shape=jax.ShapeDtypeStruct((PAIRS,), F32), in_...  64.9 us
    unnamed x11, local copies, waits for them, and re-layouts  4.28 us

profile of v1, /device:TPU:1, one launch (start us, length us, event | category | flops | bytes accessed | tf_op | source)
XLA Modules:
  0.0 69.2 jit_solution(7805284558143058328)
XLA Ops:
  0.0 0.0 copy-start
  0.0 1.0 %copy-done = bf16[1536,128]{1,0:T(8,128)(2,1)S(1)} copy-done((bf16[1536,128]{1,0:T(8,128)(2,1)S(1)}, bf16[1536,128]{1,0:T(8,128)(2,1)}, u32[]{:S(2)}) %copy-start) | copy-done | bytes 393240
  1.0 0.0 copy-start.1
  1.0 0.7 %copy-done.1 = s32[1536]{0:T(1024)S(1)} copy-done((s32[1536]{0:T(1024)S(1)}, s32[1536]{0:T(1024)}, u32[]{:S(2)}) %copy-start.1) | copy-done | bytes 6168
  1.7 0.0 copy-start.2
  1.7 0.7 %copy-done.2 = s32[1536]{0:T(1024)S(1)} copy-done((s32[1536]{0:T(1024)S(1)}, s32[1536]{0:T(1024)}, u32[]{:S(2)}) %copy-start.2) | copy-done | bytes 6168
  2.4 0.0 copy-start.3
  2.4 0.7 copy-done.3
  3.0 0.0 copy-start.4
  3.0 0.7 copy-done.4
  3.7 64.9 %shard_map.55 = f32[384]{0:T(512)S(1)} custom-call(bf16[1536,128]{1,0:T(8,128)(2,1)S(1)} %copy-done, s32[1,32]{1,0:T(1,128)S(1)} %copy-done.3, s32[64]{0:T(128)S(1)} %copy-done.4, s32[1536]{0:T(1024)S(1)} %copy-done.1, s32[1536]{0:T(1024)S(1)} %copy-done.2), custom_call_target="tpu_custom_call" | custom-call | tf_op jit(solution)/shard_map/pallas_call | solution.py:322
  68.6 0.6 copy.7
Async XLA Ops:
  0.0 1.0 %copy-start = (bf16[1536,128]{1,0:T(8,128)(2,1)S(1)}, bf16[1536,128]{1,0:T(8,128)(2,1)}, u32[]{:S(2)}) copy-start(bf16[1536,128]{1,0:T(8,128)(2,1)} %x_ref.1) | copy-start | bytes 1179652
  1.0 0.7 %copy-start.1 = (s32[1536]{0:T(1024)S(1)}, s32[1536]{0:T(1024)}, u32[]{:S(2)}) copy-start(s32[1536]{0:T(1024)} %local_ref.1) | copy-start | bytes 18436
  1.7 0.7 %copy-start.2 = (s32[1536]{0:T(1024)S(1)}, s32[1536]{0:T(1024)}, u32[]{:S(2)}) copy-start(s32[1536]{0:T(1024)} %slot_ref.1) | copy-start | bytes 18436
  2.4 0.7 copy-start.3
  3.0 0.7 copy-start.4

commit v2 on v0

v2 whole, which is shorter than its diff:
```python
import jax
import jax.numpy as jnp
from jax import lax
from jax.experimental import pallas as pl
from jax.experimental.pallas import tpu as pltpu
from jax.sharding import PartitionSpec as P

MAXAT = 128
ATOMS_DEV = 1536
STRUCTS = 32
F = 4
NY, NZ, NC = 4, 8, 2
FEATS = 128
DEPTH = F * FEATS
ROWS = ATOMS_DEV // F
TILE = MAXAT // F
SPOTS = NY * NC
WIDE = 512
PAIRS = 384
MESH = pl.DeviceIdType.MESH
BF16, F32 = jnp.bfloat16, jnp.float32

NEAR = [(dy, dc) for dy in range(NY) for dc in range(NC)]
PLANES = (0, 1, 7, 2, 6, 3, 5, 4)
EARLY = 5
BLOCKS = (0, 1, 3, 2)
NT = (((1,), (1,)), ((), ()))


def iota(shape, dim):
    return lax.broadcasted_iota(jnp.int32, shape, dim)


def fiota(shape, dim):
    return iota(shape, dim).astype(F32)


def dot(a, b):
    return jnp.dot(a, b, preferred_element_type=F32)


def split3(x):
    high = x.astype(BF16)
    rest = x - high.astype(F32)
    middle = rest.astype(BF16)
    return high, middle, (rest - middle.astype(F32)).astype(BF16)


def kernel(x_hbm, counts_hbm, req_hbm, local_hbm, slot_hbm, out_ref,
           x_ref, counts_ref, req_ref, local_ref, slot_ref,
           rows, ring, stage, recv, picks, info, asked, sizes, sums, inside, own_self, near_self,
           plane_self, far_self, table, tables,
           in_sem, x_send, x_recv, z_send, z_recv, a_send, a_recv, c_send, c_recv,
           y_send, y_recv, s_send, s_recv, p_send, p_recv, t_send, t_recv):
    s = lax.axis_index("struct")
    f = lax.axis_index("feat")
    y, z, c = s // (NZ * NC), lax.rem(s // NC, NZ), lax.rem(s, NC)
    ff = f.astype(F32)

    def struct_at(dz, dy, dc):
        return (lax.rem(y + dy + NY, NY) * NZ + lax.rem(z + dz + NZ, NZ)) * NC + lax.rem(c + dc, NC)

    def at(dz, dy, dc):
        return {"struct": struct_at(dz, dy, dc)}

    def feat_at(d):
        return {"feat": lax.rem(f + d, F)}

    def copy(src, dst, send, recv_sem, to):
        made = pltpu.make_async_remote_copy(
            src_ref=src, dst_ref=dst, send_sem=send, recv_sem=recv_sem, device_id=to,
            device_id_type=MESH)
        made.start()

    def await_all(like, sem):
        pltpu.make_async_copy(like, like, sem).wait()

    loads = []
    for n, (src, dst) in enumerate(((x_hbm, x_ref), (counts_hbm, counts_ref), (req_hbm, req_ref),
                                    (local_hbm, local_ref), (slot_hbm, slot_ref))):
        loads.append(pltpu.make_async_copy(src, dst, in_sem.at[n]))
        loads[-1].start()

    peers = [at(0, dy, dc) for dy, dc in NEAR[1:]] + [at(1, 0, 0), at(-1, 0, 0)]
    peers += [feat_at(d) for d in range(1, F)]
    barrier = pltpu.get_barrier_semaphore()
    for peer in peers:
        pl.semaphore_signal(barrier, inc=1, device_id=peer, device_id_type=MESH)

    step = 2 * FEATS
    part = step // F
    r, q = iota((step, step), 0), iota((step, step), 1)
    wanted = F * lax.rem(r, part) + lax.rem(r // part + f, F)
    deal = jnp.where(q == wanted, 1.0, 0.0).astype(BF16)
    loads[0].wait()
    for b in range(ATOMS_DEV // step):
        dealt = dot(deal, x_ref[b * step:(b + 1) * step, :]).astype(BF16)
        for e in range(F):
            rows[e * ROWS + b * part:e * ROWS + (b + 1) * part, 0:FEATS] = dealt[e * part:(e + 1) * part, :]

    for load in loads[1:]:
        load.wait()
    counts_row = jnp.concatenate(
        [counts_ref[...].astype(F32), jnp.zeros((1, 128 - STRUCTS), F32)], axis=1)
    req_row = jnp.concatenate(
        [req_ref[...].reshape(1, NY * NZ * NC).astype(F32), jnp.zeros((1, 64), F32)], axis=1)
    sub, lane = iota((STRUCTS, 128), 0), iota((STRUCTS, 128), 1)
    counts_col = jnp.sum(jnp.where(sub == lane, counts_row, 0.0), axis=1, keepdims=True)
    starts_row = jnp.sum(jnp.where(sub < lane, counts_col, 0.0), axis=0, keepdims=True)
    starts_col = jnp.sum(jnp.where(lane < sub, counts_row, 0.0), axis=1, keepdims=True)
    info[...] = jnp.concatenate(
        [req_row, counts_row, starts_row, jnp.zeros((5, 128), F32)], axis=0)
    sizes[0] = info[...]

    pl.semaphore_wait(barrier, len(peers))

    def columns(j):
        return pl.ds(pl.multiple_of(j * FEATS, FEATS), FEATS)

    def hop(o, to, j):
        dst = lax.rem(o + to + NZ, NZ)
        copy(ring.at[o, :, columns(j)], ring.at[dst, :, columns(j)], z_send, z_recv.at[dst, j], at(to, 0, 0))

    def hop_sizes(o, to):
        dst = lax.rem(o + to + NZ, NZ)
        copy(sizes.at[o], sizes.at[dst], c_send, c_recv.at[dst], at(to, 0, 0))

    def move(d, e):
        copy(rows.at[pl.ds((e + d) % F * ROWS, ROWS), pl.ds(0, FEATS)],
             rows.at[pl.ds(e * ROWS, ROWS), pl.ds((F - d) * FEATS, FEATS)],
             x_send, x_recv.at[F - d if e == 0 else 0], feat_at(d))

    def ask(dz, spots):
        for t in spots:
            dy, dc = NEAR[t]
            copy(info, asked.at[dz % 3 * SPOTS + t], a_send, a_recv.at[dz % 3], at(-dz, -dy, dc))

    def enter(j):
        ring[0, :, columns(j)] = rows[0:ROWS, columns(j)]
        hop(0, 1, j)
        hop(0, -1, j)

    enter(0)
    hop_sizes(0, 1)
    hop_sizes(0, -1)
    move(F - 1, 0)
    move(1, 0)
    ask(0, range(1, SPOTS))

    for j in BLOCKS[1:]:
        await_all(rows.at[pl.ds(0, ROWS), columns(j)], x_recv.at[j])
        enter(j)
        if j == BLOCKS[1]:
            move(2, 0)
        if j == BLOCKS[2]:
            for e in range(1, F):
                for d in (F - 1, 1, 2):
                    move(d, e)

    def pick(o, asks_rows):
        n = asks_rows.shape[0]
        sizes_ref = sizes.at[o]
        lanes = iota((n, 128), 1)
        asked_for = jnp.sum(jnp.where(lanes == struct_at(-o, 0, 0), asks_rows, 0.0), axis=1, keepdims=True)
        chosen = lanes.astype(F32) == asked_for
        count = jnp.sum(jnp.where(chosen, sizes_ref[1:2, :], 0.0), axis=1, keepdims=True)
        start = jnp.sum(jnp.where(chosen, sizes_ref[2:3, :], 0.0), axis=1, keepdims=True)
        begin = jnp.floor((start - ff + 3.0) * 0.25)
        end = jnp.floor((start + count - ff + 3.0) * 0.25)
        begin = jnp.broadcast_to(begin, (n, ROWS))
        end = jnp.broadcast_to(end, (n, ROWS))
        i, k = fiota((TILE, ROWS), 0), fiota((TILE, ROWS), 1)
        for t in range(n):
            chosen = (begin[t:t + 1] + i == k) & (k < end[t:t + 1])
            yield jnp.where(chosen, 1.0, 0.0).astype(BF16)

    def tile(n, t, j, to):
        part_rows = pl.ds(t * TILE, TILE)
        stage_rows = pl.ds(pl.multiple_of((n * SPOTS + t) * TILE, TILE), TILE)
        copy(stage.at[stage_rows, columns(j)], recv.at[n, part_rows, columns(j)], y_send, y_recv.at[n], to)

    def serve(o, n, j):
        made = dot(picks[o, 0:SPOTS * TILE], ring[o, :, columns(j)]).astype(BF16)
        stage[pl.ds(pl.multiple_of(n * SPOTS * TILE, TILE), SPOTS * TILE), columns(j)] = made
        recv[n, 0:TILE, columns(j)] = made[0:TILE]
        for t in range(1, SPOTS):
            tile(n, t, j, at(0, *NEAR[t]))

    def serve_far(o, down, j):
        made = dot(picks[o, SPOTS * TILE:], ring[o, :, columns(j)]).astype(BF16)
        for m in range(SPOTS // 2):
            t = 2 * m + down
            at_row = pl.multiple_of(t * TILE, TILE)
            n = NZ - 1
            stage_rows = pl.ds(pl.multiple_of(n * SPOTS * TILE + at_row, TILE), TILE)
            stage[stage_rows, columns(j)] = made[m * TILE:(m + 1) * TILE]
            copy(stage.at[stage_rows, columns(j)], recv.at[n, pl.ds(at_row, TILE), columns(j)],
                 y_send, y_recv.at[n], at(1 - 2 * down, m, down))

    def products(n):
        for b in range(ATOMS_DEV // WIDE):
            cols = slice(b * WIDE, (b + 1) * WIDE)
            p = lax.dot_general(recv[n], rows[cols, :], NT, preferred_element_type=F32)
            sums[pl.ds(pl.multiple_of(n * SPOTS, SPOTS), SPOTS), cols] = jnp.sum(
                (p * p).reshape(SPOTS, TILE, WIDE), axis=1)

    def near_products(n, carry):
        await_all(recv.at[n, pl.ds(TILE, (SPOTS - 1) * TILE)], y_recv.at[n])
        products(n)
        return carry

    def by_structure(first, last):
        return sum(
            lax.dot_general(inside[...], piece, NT, preferred_element_type=F32)
            for piece in split3(sums[first * SPOTS:last * SPOTS]))

    await_all(asked.at[pl.ds(0, SPOTS - 1)], a_recv.at[0])
    near_asks = jnp.concatenate([info[0:1, :]] + [asked[t, 0:1, :] for t in range(1, SPOTS)], axis=0)

    def pick_near(o):
        for t, chosen in enumerate(pick(o, near_asks)):
            picks[o, t * TILE:(t + 1) * TILE] = chosen

    pick_near(0)

    def own_block(j, carry):
        serve(0, 0, j)
        return carry

    lax.fori_loop(0, F, own_block, 0)

    def block_at(m):
        return jnp.where(m < 2, m, F + 1 - m)

    def next_hop(i, carry):
        hop_no, m = i // F + 1, lax.rem(i, F)
        j = block_at(m)

        def arrive(down, carry):
            o = jnp.where(down == 0, hop_no, NZ - hop_no)
            await_all(ring.at[o, :, columns(j)], z_recv.at[o, j])
            hop(o, 1 - 2 * down, j)

            @pl.when(m == 0)
            def _():
                await_all(sizes.at[o], c_recv.at[o])
                hop_sizes(o, 1 - 2 * down)
            return carry

        lax.fori_loop(0, 2, arrive, 0)

        @pl.when(i == 0)
        def _():
            ask(1, range(0, SPOTS, 2))
            ask(-1, range(1, SPOTS, 2))

        def send(down, carry):
            o = jnp.where(down == 0, hop_no, NZ - hop_no)

            @pl.when(m == 0)
            def _():
                pick_near(o)

            serve(o, 2 * hop_no - 1 + down, j)
            return carry

        lax.fori_loop(0, 2, send, 0)
        return carry

    lax.fori_loop(0, 2 * F, next_hop, 0)

    column = iota((STRUCTS, ATOMS_DEV), 1)
    e_of = sum(jnp.where(column >= n * ROWS, 1, 0) for n in range(1, F))
    index = F * (column - ROWS * e_of) + lax.rem(f + e_of, F)
    index = index.astype(F32)
    belongs = (starts_col <= index) & (index < starts_col + counts_col)
    inside[...] = jnp.where(belongs, 1.0, 0.0).astype(BF16)
    seg_row = jnp.sum(jnp.where(belongs, fiota((STRUCTS, ATOMS_DEV), 0), 0.0), axis=0, keepdims=True)
    own_row = F * fiota((ROWS, 128), 0) + ff
    own_seg = jnp.sum(
        jnp.where((starts_row + counts_row <= own_row) & (iota((ROWS, 128), 1) < STRUCTS), 1.0, 0.0),
        axis=1, keepdims=True)

    def self_kernel():
        total = jnp.zeros((STRUCTS, 1), F32)
        for b in range(ATOMS_DEV // WIDE):
            cols = slice(b * WIDE, (b + 1) * WIDE)
            p = lax.dot_general(rows[0:ROWS, :], rows[cols, :], NT, preferred_element_type=F32)
            p = jnp.where(own_seg == seg_row[:, cols], p, 0.0)
            by_column = jnp.sum(p * p, axis=0, keepdims=True)
            total = total + jnp.sum(
                jnp.where(inside[:, cols].astype(F32) > 0.5, by_column, 0.0), axis=1, keepdims=True)
        return total

    await_all(rows.at[pl.ds(ROWS, (F - 1) * ROWS), pl.ds(FEATS, (F - 1) * FEATS)], x_recv.at[0])
    self_col = self_kernel()
    own_self[...] = jnp.broadcast_to(
        jnp.sum(jnp.where(sub == lane, self_col, 0.0), axis=0, keepdims=True), (8, 128))
    for t in range(1, SPOTS):
        copy(own_self, near_self.at[t], s_send, s_recv, at(0, *NEAR[t]))

    def spread_self():
        await_all(near_self.at[pl.ds(1, SPOTS - 1)], s_recv)
        plane_self[...] = jnp.concatenate(
            [own_self[0:1, :]] + [near_self[t, 0:1, :] for t in range(1, SPOTS)], axis=0)
        for o in range(1, NZ):
            copy(plane_self, far_self.at[o], p_send, p_recv, at(o, 0, 0))

    def last_hop(m, carry):
        j = block_at(m)

        def send(down, carry):
            o = jnp.where(down == 0, 3, NZ - 3)
            await_all(ring.at[o, :, columns(j)], z_recv.at[o, j])

            @pl.when(m == 0)
            def _():
                await_all(sizes.at[o], c_recv.at[o])
                pick_near(o)
                await_all(asked.at[pl.ds(0, SPOTS // 2)], a_recv.at[1 + down])
                far_asks = jnp.concatenate(
                    [asked[(1 + down) * SPOTS + 2 * t + down, 0:1, :] for t in range(SPOTS // 2)], axis=0)
                for t, chosen in enumerate(pick(o, far_asks)):
                    picks[o, (SPOTS + t) * TILE:(SPOTS + t + 1) * TILE] = chosen

            serve_far(o, down, j)
            serve(o, 5 + down, j)
            return carry

        lax.fori_loop(0, 2, send, 0)

        @pl.when(m == 1)
        def _():
            spread_self()

        return carry

    lax.fori_loop(0, F, last_hop, 0)

    lax.fori_loop(0, EARLY, near_products, 0)
    early = by_structure(0, EARLY)

    def holder_of(spot):
        n = spot // SPOTS
        t = lax.rem(spot, SPOTS)
        o = sum(jnp.where(n == m, plane, 0) for m, plane in enumerate(PLANES))
        return (lax.rem(y - t // NC + NY, NY) * NZ + lax.rem(z - o + NZ, NZ)) * NC + lax.rem(
            c + lax.rem(t, NC), NC)

    holders = NZ * SPOTS
    spot, lanes = iota((holders, 128), 0), iota((holders, 128), 1)
    my_request = jnp.sum(jnp.where(lanes == holder_of(spot), info[0:1, :], 0.0), axis=1, keepdims=True)
    await_all(far_self.at[pl.ds(1, NZ - 1)], p_recv)
    all_self = jnp.concatenate([far_self[o] if o else plane_self[...] for o in PLANES], axis=0)
    partner_self = jnp.sum(jnp.where(lanes.astype(F32) == my_request, all_self, 0.0), axis=1, keepdims=True)
    partner_row = jnp.sum(jnp.where(lanes == spot, partner_self, 0.0), axis=0, keepdims=True)
    table[STRUCTS:STRUCTS + 8, :] = jnp.broadcast_to(partner_row, (8, 128))

    pairs = pl.ds(pl.multiple_of(f * PAIRS, 128), PAIRS)
    spot = iota((128, PAIRS), 0)
    slot_pick = jnp.where(
        (holder_of(spot) == slot_ref[pairs].reshape(1, PAIRS)) & (spot < holders), 1.0, 0.0).astype(BF16)
    local_pick = iota((STRUCTS, PAIRS), 0) == local_ref[pairs].reshape(1, PAIRS)

    lax.fori_loop(EARLY, NZ - 1, near_products, 0)
    await_all(recv.at[NZ - 1], y_recv.at[NZ - 1])
    products(NZ - 1)
    late = by_structure(EARLY, NZ)
    table[0:STRUCTS, :] = jnp.concatenate(
        [early, late, jnp.broadcast_to(self_col, (STRUCTS, 128 - holders))], axis=1)
    for d in range(1, F):
        copy(table, tables.at[d - 1], t_send, t_recv, feat_at(d))
    await_all(rows.at[:, pl.ds(FEATS, (F - 1) * FEATS)], x_send)
    await_all(ring.at[pl.ds(0, 6)], z_send)
    await_all(sizes.at[pl.ds(0, 6)], c_send)
    await_all(asked.at[pl.ds(0, 2 * SPOTS - 1)], a_send)
    await_all(stage.at[pl.ds(0, ((NZ - 1) * (SPOTS - 1) + SPOTS) * TILE)], y_send)
    await_all(near_self.at[pl.ds(0, SPOTS - 1)], s_send)
    await_all(far_self.at[pl.ds(0, NZ - 1)], p_send)
    await_all(tables, t_recv)
    await_all(tables, t_send)
    total = (table[...] + tables[0]) + (tables[1] + tables[2])
    picked = sum(dot(piece, slot_pick) for piece in split3(total))
    left_self = jnp.sum(jnp.where(local_pick, total[0:STRUCTS, holders:holders + 1], 0.0), axis=0, keepdims=True)
    value = jnp.sum(jnp.where(local_pick, picked[0:STRUCTS], 0.0), axis=0, keepdims=True)
    right_self = picked[STRUCTS:STRUCTS + 1]
    out_ref[...] = (value / jnp.sqrt(left_self * right_self)).reshape(PAIRS)


def per_device(descriptors, atom_counts, partner_requests, pair_local, pair_slot):
    dma = pltpu.SemaphoreType.DMA
    vmem = pltpu.VMEM

    inputs = (descriptors, atom_counts, partner_requests, pair_local, pair_slot)
    return pl.pallas_call(
        kernel,
        out_shape=jax.ShapeDtypeStruct((PAIRS,), F32),
        in_specs=[pl.BlockSpec(memory_space=pl.ANY)] * 5,
        out_specs=pl.BlockSpec(memory_space=vmem),
        scratch_shapes=[
            *[vmem(a.shape, a.dtype) for a in inputs],
            vmem((ATOMS_DEV, DEPTH), BF16),
            vmem((NZ, ROWS, DEPTH), BF16),
            vmem((NZ * SPOTS * TILE, DEPTH), BF16),
            vmem((NZ, SPOTS * TILE, DEPTH), BF16),
            vmem((NZ, (SPOTS + SPOTS // 2) * TILE, ROWS), BF16),
            vmem((8, 128), F32),
            vmem((3 * SPOTS, 8, 128), F32),
            vmem((NZ, 8, 128), F32),
            vmem((NZ * SPOTS, ATOMS_DEV), F32),
            vmem((STRUCTS, ATOMS_DEV), BF16),
            vmem((8, 128), F32),
            vmem((SPOTS, 8, 128), F32),
            vmem((8, 128), F32),
            vmem((NZ, 8, 128), F32),
            vmem((STRUCTS + 8, 128), F32),
            vmem((F - 1, STRUCTS + 8, 128), F32),
            dma((5,)),
            dma(()), dma((F,)),
            dma(()), dma((NZ, F)),
            dma(()), dma((3,)),
            dma(()), dma((NZ,)),
            dma(()), dma((NZ,)),
            dma(()), dma(()),
            dma(()), dma(()),
            dma(()), dma(()),
        ],
        compiler_params=pltpu.CompilerParams(
            collective_id=0, has_side_effects=True, vmem_limit_bytes=62 * 1024 * 1024),
    )(*inputs)


def solution(mesh):
    in_specs = (P("struct", "feat"), P("struct", None), P("struct"), P("struct"), P("struct"))
    out_specs = P(("struct", "feat"))
    return jax.shard_map(
        per_device, mesh=mesh, in_specs=in_specs, out_specs=out_specs, check_vma=False)
```

time: 313 us -> 54 us (0.17)
  local copies, waits for them, and re-layouts: 82.5 us -> 1.26 us
  waiting for transfers between devices: 79 us -> 0 us
  blocking collectives: 78.2 us -> 0 us
  Pallas kernels: 0 us -> 52.6 us
  matrix products: 51.9 us -> 0 us
  between operations: 13.5 us -> 0.01 us
  other arithmetic: 7.09 us -> 0 us
    gather x8 -> x0, local copies, waits for them, and re-layouts: 80.6 us -> none  [the longest x3 35 us: block_sums(): right_tiles = jnp.take(partner, index_pair[1], axis=0)]
    all_gather x2 -> x0, waiting for transfers between devices: 79 us -> none  [the longest x1 79 us: per_device(): partner = lax.all_gather(partner, 'feat', axis=2, tiled=True)]
    all_to_all x2 -> x0, blocking collectives: 78.2 us -> none  [the longest x1 56 us: per_device(): lax.all_to_all(packed, 'struct', split_axis=0, concat_axis=0, tiled=True)]
    pallas_call x0 -> x1, Pallas kernels: none -> 52.6 us  [per_device(): pl.pallas_call(kernel, out_shape=jax.ShapeDtypeStruct((PAIRS,), F32), in_...]
    dot_general x5 -> x0, matrix products: 51.9 us -> none  [gram_tiles(): jnp.einsum('amd,and->amn', left_rows, right_rows, preferred_element_type=...]
  transfers between devices with their start and end apart: 2 -> 0, of which waited for: 1 -> 0; matrix products, arithmetic and copies ran while one was open for 3% -> 0% of each run, Pallas kernels for 0% -> 0%
where the time goes in v2:
time: 54 us; the launch traced here: 53.9 us
  Pallas kernels  52.6 us (97%)
  local copies, waits for them, and re-layouts  1.26 us (2%)
    pallas_call x1, Pallas kernels, per_device(): pl.pallas_call(kernel, out_shape=jax.ShapeDtypeStruct((PAIRS,), F32), in_...  52.6 us
    unnamed x1, local copies, waits for them, and re-layouts  1.26 us

profile of v2, /device:TPU:1, one launch (start us, length us, event | category | flops | bytes accessed | tf_op | source)
XLA Modules:
  0.0 53.9 jit_solution(4468848869044281207)
XLA Ops:
  0.0 52.6 %shard_map.55 = f32[384]{0:T(512)} custom-call(bf16[1536,128]{1,0:T(8,128)(2,1)} %x_hbm.1, s32[1,32]{1,0:T(1,128)} %counts_hbm.1, s32[64]{0:T(128)} %req_hbm.1, s32[1536]{0:T(1024)} %local_hbm.1, s32[1536]{0:T(1024)} %slot_hbm.1), custom_call_target="tpu_custom_call" | custom-call | tf_op jit(solution)/shard_map/pallas_call | solution.py:395
  52.6 1.3 %copy.7 = f32[384]{0:T(512)} copy(f32[384]{0:T(512)} %shard_map.55) | data formatting | bytes 3072

commit v3 on v2

--- a/solution.py
+++ b/solution.py
@@ -50,7 +50,7 @@
            x_ref, counts_ref, req_ref, local_ref, slot_ref,
            rows, ring, stage, recv, picks, info, asked, sizes, sums, inside, own_self, near_self,
            plane_self, far_self, table, tables,
-           in_sem, x_send, x_recv, z_send, z_recv, a_send, a_recv, c_send, c_recv,
+           in_sem, xh_recv, x_send, x_recv, z_send, z_recv, a_send, a_recv, c_send, c_recv,
            y_send, y_recv, s_send, s_recv, p_send, p_recv, t_send, t_recv):
     s = lax.axis_index("struct")
     f = lax.axis_index("feat")
@@ -130,6 +130,20 @@
              rows.at[pl.ds(e * ROWS, ROWS), pl.ds((F - d) * FEATS, FEATS)],
              x_send, x_recv.at[F - d if e == 0 else 0], feat_at(d))
 
+    def halves(half):
+        return pl.ds(half * ROWS // 4, ROWS // 4)
+
+    def move_half(d, half):
+        copy(rows.at[pl.ds(d * ROWS + half * ROWS // 4, ROWS // 4), pl.ds(0, FEATS)],
+             rows.at[halves(half), pl.ds((F - d) * FEATS, FEATS)],
+             x_send, xh_recv.at[F - d, half], feat_at(d))
+
+    def enter_half(j, half):
+        ring[0, halves(half), columns(j)] = rows[halves(half), columns(j)]
+        for to in (1, NZ - 1):
+            copy(ring.at[0, halves(half), columns(j)], ring.at[to, halves(half), columns(j)],
+                 z_send, z_recv.at[to, j], at(1 if to == 1 else -1, 0, 0))
+
     def ask(dz, spots):
         for t in spots:
             dy, dc = NEAR[t]
@@ -143,15 +157,20 @@
     enter(0)
     hop_sizes(0, 1)
     hop_sizes(0, -1)
-    move(F - 1, 0)
-    move(1, 0)
+    for half in range(4):
+        move_half(F - 1, half)
+        move_half(1, half)
+    move(2, 0)
     ask(0, range(1, SPOTS))
 
     for j in BLOCKS[1:]:
-        await_all(rows.at[pl.ds(0, ROWS), columns(j)], x_recv.at[j])
-        enter(j)
-        if j == BLOCKS[1]:
-            move(2, 0)
+        if j == 2:
+            await_all(rows.at[pl.ds(0, ROWS), columns(j)], x_recv.at[j])
+            enter(j)
+        else:
+            for half in range(4):
+                await_all(rows.at[halves(half), columns(j)], xh_recv.at[j, half])
+                enter_half(j, half)
         if j == BLOCKS[2]:
             for e in range(1, F):
                 for d in (F - 1, 1, 2):
@@ -329,7 +348,7 @@
 
         lax.fori_loop(0, 2, send, 0)
 
-        @pl.when(m == 1)
+        @pl.when(m == 3)
         def _():
             spread_self()
 
@@ -415,7 +434,7 @@
             vmem((NZ, 8, 128), F32),
             vmem((STRUCTS + 8, 128), F32),
             vmem((F - 1, STRUCTS + 8, 128), F32),
-            dma((5,)),
+            dma((5,)), dma((F, 4)),
             dma(()), dma((F,)),
             dma(()), dma((NZ, F)),
             dma(()), dma((3,)),

time: 54 us -> 52.2 us (0.967)
  Pallas kernels: 52.6 us -> 50.8 us
    pallas_call x1, Pallas kernels: 52.6 us -> 50.8 us  [per_device(): pl.pallas_call(kernel, out_shape=jax.ShapeDtypeStruct((PAIRS,), F32), in_...]
where the time goes in v3:
time: 52.2 us; the launch traced here: 52 us
  Pallas kernels  50.8 us (97%)
  local copies, waits for them, and re-layouts  1.26 us (2%)
    pallas_call x1, Pallas kernels, per_device(): pl.pallas_call(kernel, out_shape=jax.ShapeDtypeStruct((PAIRS,), F32), in_...  50.8 us
    unnamed x1, local copies, waits for them, and re-layouts  1.26 us

profile of v3, /device:TPU:1, one launch (start us, length us, event | category | flops | bytes accessed | tf_op | source)
XLA Modules:
  0.0 52.0 jit_solution(6354009164458363881)
XLA Ops:
  0.0 50.8 %shard_map.55 = f32[384]{0:T(512)} custom-call(bf16[1536,128]{1,0:T(8,128)(2,1)} %x_hbm.1, s32[1,32]{1,0:T(1,128)} %counts_hbm.1, s32[64]{0:T(128)} %req_hbm.1, s32[1536]{0:T(1024)} %local_hbm.1, s32[1536]{0:T(1024)} %slot_hbm.1), custom_call_target="tpu_custom_call" | custom-call | tf_op jit(solution)/shard_map/pallas_call | solution.py:414
  50.8 1.3 %copy.7 = f32[384]{0:T(512)} copy(f32[384]{0:T(512)} %shard_map.55) | data formatting | bytes 3072

commit v4 on v3

--- a/solution.py
+++ b/solution.py
@@ -248,46 +248,6 @@
 
     lax.fori_loop(0, F, own_block, 0)
 
-    def block_at(m):
-        return jnp.where(m < 2, m, F + 1 - m)
-
-    def next_hop(i, carry):
-        hop_no, m = i // F + 1, lax.rem(i, F)
-        j = block_at(m)
-
-        def arrive(down, carry):
-            o = jnp.where(down == 0, hop_no, NZ - hop_no)
-            await_all(ring.at[o, :, columns(j)], z_recv.at[o, j])
-            hop(o, 1 - 2 * down, j)
-
-            @pl.when(m == 0)
-            def _():
-                await_all(sizes.at[o], c_recv.at[o])
-                hop_sizes(o, 1 - 2 * down)
-            return carry
-
-        lax.fori_loop(0, 2, arrive, 0)
-
-        @pl.when(i == 0)
-        def _():
-            ask(1, range(0, SPOTS, 2))
-            ask(-1, range(1, SPOTS, 2))
-
-        def send(down, carry):
-            o = jnp.where(down == 0, hop_no, NZ - hop_no)
-
-            @pl.when(m == 0)
-            def _():
-                pick_near(o)
-
-            serve(o, 2 * hop_no - 1 + down, j)
-            return carry
-
-        lax.fori_loop(0, 2, send, 0)
-        return carry
-
-    lax.fori_loop(0, 2 * F, next_hop, 0)
-
     column = iota((STRUCTS, ATOMS_DEV), 1)
     e_of = sum(jnp.where(column >= n * ROWS, 1, 0) for n in range(1, F))
     index = F * (column - ROWS * e_of) + lax.rem(f + e_of, F)
@@ -299,6 +259,46 @@
     own_seg = jnp.sum(
         jnp.where((starts_row + counts_row <= own_row) & (iota((ROWS, 128), 1) < STRUCTS), 1.0, 0.0),
         axis=1, keepdims=True)
+
+    def block_at(m):
+        return jnp.where(m < 2, m, F + 1 - m)
+
+    def next_hop(i, carry):
+        hop_no, m = i // F + 1, lax.rem(i, F)
+        j = block_at(m)
+
+        def arrive(down, carry):
+            o = jnp.where(down == 0, hop_no, NZ - hop_no)
+            await_all(ring.at[o, :, columns(j)], z_recv.at[o, j])
+            hop(o, 1 - 2 * down, j)
+
+            @pl.when(m == 0)
+            def _():
+                await_all(sizes.at[o], c_recv.at[o])
+                hop_sizes(o, 1 - 2 * down)
+            return carry
+
+        lax.fori_loop(0, 2, arrive, 0)
+
+        @pl.when(i == 0)
+        def _():
+            ask(1, range(0, SPOTS, 2))
+            ask(-1, range(1, SPOTS, 2))
+
+        def send(down, carry):
+            o = jnp.where(down == 0, hop_no, NZ - hop_no)
+
+            @pl.when(m == 0)
+            def _():
+                pick_near(o)
+
+            serve(o, 2 * hop_no - 1 + down, j)
+            return carry
+
+        lax.fori_loop(0, 2, send, 0)
+        return carry
+
+    lax.fori_loop(0, 2 * F, next_hop, 0)
 
     def self_kernel():
         total = jnp.zeros((STRUCTS, 1), F32)

time: 52.2 us -> 52.2 us (level)
  no operation moved by 1% of the time
where the time goes in v4:
time: 52.2 us; the launch traced here: 52 us
  Pallas kernels  50.8 us (97%)
  local copies, waits for them, and re-layouts  1.26 us (2%)
    pallas_call x1, Pallas kernels, per_device(): pl.pallas_call(kernel, out_shape=jax.ShapeDtypeStruct((PAIRS,), F32), in_...  50.8 us
    unnamed x1, local copies, waits for them, and re-layouts  1.26 us

profile of v4, /device:TPU:1, one launch (start us, length us, event | category | flops | bytes accessed | tf_op | source)
XLA Modules:
  0.0 52.0 jit_solution(1831583070031527405)
XLA Ops:
  0.0 50.8 %shard_map.55 = f32[384]{0:T(512)} custom-call(bf16[1536,128]{1,0:T(8,128)(2,1)} %x_hbm.1, s32[1,32]{1,0:T(1,128)} %counts_hbm.1, s32[64]{0:T(128)} %req_hbm.1, s32[1536]{0:T(1024)} %local_hbm.1, s32[1536]{0:T(1024)} %slot_hbm.1), custom_call_target="tpu_custom_call" | custom-call | tf_op jit(solution)/shard_map/pallas_call | solution.py:414
  50.8 1.3 %copy.7 = f32[384]{0:T(512)} copy(f32[384]{0:T(512)} %shard_map.55) | data formatting | bytes 3072
